TPU v7x, 256 devices: a whole 4x4x8 slice. The times are simulated.
256 devices in a mesh: req: 8 (over z), ctx: 32 (over x, y, core).
Axes of the slice: x: 4, y: 4, z: 8, core: 2. Of those that a mesh axis runs over, the one named last changes fastest.
Arguments:
- prompt_key_value: bfloat16 [32768, 2048], P('ctx'), may hold values from -6 to 6
- suffix_key_value: bfloat16 [128, 1024, 2048], P('req', 'ctx'), may hold values from -8 to 8
- roots: int32 [128], replicated, may hold values from 0 to 127, as said below
- parents: int32 [3, 128], P(None, 'req'), may hold values from 0 to 15
- block_mask: int32 [128, 8], P('req'), may hold values 0 or 1
- queries: bfloat16 [4, 128, 8192], P(None, 'req', 'ctx'), may hold values from -470 to 470
- draft_kv: bfloat16 [4, 128, 2048], P(None, 'req'), may hold values from -6 to 6
Outputs:
- attention: bfloat16 [4, 128, 8192], P(None, 'req', 'ctx')
Inputs may be any that keep to these rules, and one draw needn't show every extreme that they name: The 16 step-0 particles of req index d (d * 16 to d * 16 + 15) contain exactly 2 whose roots r lie on each req index r // 16.
All inputs are finite; a program needn't handle non-finite values. No bound on the sum of `block_mask` on one device may be relied on, other than what follows from the above.
Results may differ from a plain program's by a relative error of at most 0.0034.
Values may be sent and summed in bfloat16 or wider, within the bound.
A program may use at most 192 MiB of HBM per device.

v0:
```python
import math

import jax
import jax.numpy as jnp
from jax import lax
from jax.sharding import PartitionSpec as P

QUERY_HEAD_COUNT = 64
KEY_VALUE_HEADS = 8
HEAD_SIZE = 128
DRAFT_STEPS = 4
BLK = 128


masked_score = -1e30


def trace_lineage(parents, particles):
    layers_all = []
    for target in range(DRAFT_STEPS):
        current = particles
        columns = [particles] * DRAFT_STEPS
        for back in range(target - 1, -1, -1):
            current = jnp.take(parents[back], current)
            columns[back] = current
        layers_all.append(jnp.stack(columns))
    return jnp.stack(layers_all)


def body(prompt_key_value, suffix_key_value, roots, parents, block_mask, queries, draft_kv):
    req_count = lax.axis_size("req")
    ctx_count = lax.axis_size("ctx")
    req_index = lax.axis_index("req")
    ctx_index = lax.axis_index("ctx")
    per_req = suffix_key_value.shape[0]
    tok_span = suffix_key_value.shape[1]
    key_value_width = KEY_VALUE_HEADS * HEAD_SIZE
    query_group_size = QUERY_HEAD_COUNT // KEY_VALUE_HEADS
    slot_count = per_req // req_count
    local_heads = QUERY_HEAD_COUNT // ctx_count
    total_row_count = DRAFT_STEPS * per_req
    score_scale = 1.0 / math.sqrt(HEAD_SIZE)
    gathered_suffix = lax.all_gather(queries, "ctx", axis=2, tiled=True)
    route_table = roots.reshape(req_count, per_req)
    anchors = route_table // per_req
    is_mine = (anchors == req_index).astype(jnp.int32)
    slot_rank = jnp.cumsum(is_mine, axis=1) - 1
    slot_ids = jnp.arange(slot_count, dtype=jnp.int32)
    chosen = (is_mine[:, None, :] > 0) & (slot_rank[:, None, :] == slot_ids[None, :, None])
    picked = jnp.sum(jnp.where(chosen, (route_table % per_req)[:, None, :], 0), axis=2)
    outgoing = jnp.take(suffix_key_value, picked.reshape(-1), axis=0).reshape(
        req_count, slot_count, tok_span, 2 * key_value_width
    )
    incoming = lax.all_to_all(outgoing, "req", split_axis=0, concat_axis=0, tiled=True)
    own_roots = lax.dynamic_slice_in_dim(roots, req_index * per_req, per_req)
    own_anchor = own_roots // per_req
    particles = jnp.arange(per_req, dtype=jnp.int32)
    earlier = (own_anchor[None, :] == own_anchor[:, None]) & (
        particles[None, :] < particles[:, None]
    )
    own_rank = jnp.sum(earlier.astype(jnp.int32), axis=1)
    resident = jnp.take(
        incoming.reshape(req_count * slot_count, tok_span, 2 * key_value_width),
        own_anchor * slot_count + own_rank,
        axis=0,
    )
    lineage = trace_lineage(parents, particles)
    first_step = lineage[:, 0, :].reshape(total_row_count)
    block_ids = (ctx_index * tok_span + jnp.arange(tok_span, dtype=jnp.int32)) // BLK
    live_tokens = jnp.take(jnp.take(block_mask, first_step, axis=0), block_ids, axis=1) > 0
    query_matrix = gathered_suffix.reshape(
        total_row_count, KEY_VALUE_HEADS, query_group_size, HEAD_SIZE
    )
    peaks = []
    totals = []
    accums = []
    for current_head_index in range(KEY_VALUE_HEADS):
        key_start = current_head_index * HEAD_SIZE
        value_start = key_value_width + key_start
        query_head = query_matrix[:, current_head_index]
        key_prompt = prompt_key_value[:, key_start : key_start + HEAD_SIZE]
        value_prompt = prompt_key_value[:, value_start : value_start + HEAD_SIZE]
        score_prompt = (
            jnp.einsum("qgd,nd->qgn", query_head, key_prompt, preferred_element_type=jnp.float32)
            * score_scale
        )
        key_suffix = jnp.take(resident[:, :, key_start : key_start + HEAD_SIZE], first_step, axis=0)
        value_suffix = jnp.take(
            resident[:, :, value_start : value_start + HEAD_SIZE], first_step, axis=0
        )
        score_suffix = (
            jnp.einsum("qgd,qnd->qgn", query_head, key_suffix, preferred_element_type=jnp.float32)
            * score_scale
        )
        score_suffix = jnp.where(live_tokens[:, None, :], score_suffix, masked_score)
        highest = jnp.maximum(jnp.max(score_prompt, axis=2), jnp.max(score_suffix, axis=2))
        weight_prompt = jnp.exp(score_prompt - highest[..., None])
        weight_suffix = jnp.exp(score_suffix - highest[..., None])
        totals.append(jnp.sum(weight_prompt, axis=2) + jnp.sum(weight_suffix, axis=2))
        accum_head = jnp.einsum(
            "qgn,nd->qgd",
            weight_prompt.astype(jnp.bfloat16),
            value_prompt,
            preferred_element_type=jnp.float32,
        )
        accum_head = accum_head + jnp.einsum(
            "qgn,qnd->qgd",
            weight_suffix.astype(jnp.bfloat16),
            value_suffix,
            preferred_element_type=jnp.float32,
        )
        accums.append(accum_head)
        peaks.append(highest)
    peak_rows = jnp.stack(peaks, axis=1).reshape(total_row_count, QUERY_HEAD_COUNT)
    total_rows = jnp.stack(totals, axis=1).reshape(total_row_count, QUERY_HEAD_COUNT)
    accum_rows = jnp.stack(accums, axis=1).reshape(total_row_count, QUERY_HEAD_COUNT, HEAD_SIZE)
    head_start = ctx_index * local_heads
    peak_all = lax.pmax(peak_rows, "ctx")
    factor = jnp.exp(peak_rows - peak_all)
    own_total, own_accum = (
        lax.psum_scatter(total_rows * factor, "ctx", scatter_dimension=1, tiled=True),
        lax.psum_scatter(accum_rows * factor[..., None], "ctx", scatter_dimension=1, tiled=True),
    )
    own_peak = lax.dynamic_slice_in_dim(peak_all, head_start, local_heads, 1)
    draft_token_rows = draft_kv[jnp.arange(DRAFT_STEPS, dtype=jnp.int32)[None, :, None], lineage]
    draft_token_rows = jnp.transpose(draft_token_rows, (0, 2, 1, 3)).reshape(
        total_row_count, DRAFT_STEPS, 2, KEY_VALUE_HEADS, HEAD_SIZE
    )
    head_ids = head_start + jnp.arange(local_heads, dtype=jnp.int32)
    draft_heads = jnp.take(draft_token_rows, head_ids // query_group_size, axis=3)
    query_own = queries.reshape(total_row_count, local_heads, HEAD_SIZE)
    score_draft = (
        jnp.einsum(
            "qhd,qshd->qhs", query_own, draft_heads[:, :, 0], preferred_element_type=jnp.float32
        )
        * score_scale
    )
    step_of = jnp.arange(total_row_count, dtype=jnp.int32) // per_req
    allowed = jnp.arange(DRAFT_STEPS, dtype=jnp.int32)[None, :] <= step_of[:, None]
    score_draft = jnp.where(allowed[:, None, :], score_draft, masked_score)
    highest = jnp.maximum(own_peak, jnp.max(score_draft, axis=2))
    carried = jnp.exp(own_peak - highest)
    weight_draft = jnp.exp(score_draft - highest[..., None])
    denominator = own_total * carried + jnp.sum(weight_draft, axis=2)
    numerator = own_accum * carried[..., None] + jnp.einsum(
        "qhs,qshd->qhd",
        weight_draft.astype(jnp.bfloat16),
        draft_heads[:, :, 1],
        preferred_element_type=jnp.float32,
    )
    result = (numerator / denominator[..., None]).astype(jnp.bfloat16)
    return result.reshape(DRAFT_STEPS, per_req, local_heads * HEAD_SIZE)


def solution(mesh):
    return jax.shard_map(
        body,
        mesh=mesh,
        in_specs=(
            P("ctx", None),
            P("req", "ctx", None),
            P(),
            P(None, "req"),
            P("req", None),
            P(None, "req", "ctx"),
            P(None, "req", None),
        ),
        out_specs=P(None, "req", "ctx"),
        check_vma=False,
    )
```

profile of v0, /device:TPU:1, one launch (start us, length us, event | category | flops | bytes accessed | tf_op | source)
XLA Modules:
  0.0 471.9 jit_solution(6605967080224694059)
XLA Ops:
  11.1 3.2 broadcast_select_fusion.1
  14.3 9.1 %all-to-all-start = ((bf16[8,2,32,2048]{3,2,1,0:T(8,128)(2,1)}), bf16[8,2,32,2048]{3,2,1,0:T(8,128)(2,1)}, u32[]{:S(2)}, u32[]{:S(2)}) async-start(bf16[8,2,32,2048]{3,2,1,0:T(8,128)(2,1)} %bitcast.307), calls=%async_computation | async-start | bytes 4194304 | tf_op jit(solution)/shard_map/all_to_all | solution.py:54
  32.2 29.9 %all-gather.2.cloned.1.call-done = bf16[4,16,8192]{2,1,0:T(8,128)(2,1)} async-done(((bf16[4,16,256]{2,1,0:T(8,128)(2,1)}), bf16[4,16,8192]{2,1,0:T(8,128)(2,1)}) %all-gather.2.cloned.1.call-update) | async-done | bytes 1048592 | tf_op jit(solution)/shard_map/all_gather | solution.py:43
  63.6 3.3 multiply_reduce_fusion.1
  66.9 3.4 multiply_reduce_fusion.2
  70.3 3.3 multiply_reduce_fusion.3
  73.6 3.4 multiply_reduce_fusion.4
  76.9 3.3 multiply_reduce_fusion.5
  80.3 3.3 multiply_reduce_fusion.6
  83.6 3.3 multiply_reduce_fusion.7
  86.9 3.3 multiply_reduce_fusion
  90.3 3.6 gather_fusion.11
  102.5 2.7 fusion.12
  112.8 2.7 fusion.10
  123.2 2.7 fusion.8
  133.6 2.7 fusion.6
  144.1 2.7 fusion.4
  154.4 2.7 fusion.2
  164.8 2.7 fusion
  175.1 2.7 fusion.14
  198.5 121.1 %pmax.7 = f32[64,64]{0,1:T(8,128)S(1)} all-reduce(f32[64,64]{0,1:T(8,128)S(1)} %bitcast.336), channel_id=1, replica_groups=mesh['req'=8,'ctx'=32] {'ctx'}, use_global_device_ids=true, to_apply=%region_19.23 | all-reduce | flops 4096 | bytes 32768 | tf_op jit(solution)/shard_map/pmax | solution.py:118
  327.4 2.6 copy.148
  331.5 4.3 gather_fusion.2
  339.2 123.9 %all-reduce = f32[64,64]{0,1:T(8,128)S(1)} all-reduce(f32[64,64]{0,1:T(8,128)S(1)} %get-tuple-element.10), channel_id=3, replica_groups=mesh['req'=8,'ctx'=32] {'ctx'}, use_global_device_ids=true, to_apply=%region_38.42.clone | all-reduce | flops 4096 | bytes 32768
  (332 shorter events, 110.8 us)
Async XLA Ops:
  6.5 55.5 %all-gather.2.cloned.1.call-start = ((), (), s32[]{:S(2)}) async-start(), calls=%async_computation.2 | async-start | bytes 1081344 | tf_op jit(solution)/shard_map/all_gather | solution.py:43
  14.3 9.2 %copy-start.69 = (s32[3,16]{1,0:T(4,128)S(1)}, s32[3,16]{1,0:T(4,128)}, u32[]{:S(2)}) copy-start(s32[3,16]{1,0:T(4,128)} %param.16) | copy-start | bytes 580
  14.3 76.0 %all-to-all-start = ((bf16[8,2,32,2048]{3,2,1,0:T(8,128)(2,1)}), bf16[8,2,32,2048]{3,2,1,0:T(8,128)(2,1)}, u32[]{:S(2)}, u32[]{:S(2)}) async-start(bf16[8,2,32,2048]{3,2,1,0:T(8,128)(2,1)} %bitcast.307), calls=%async_computation | async-start | bytes 4194304 | tf_op jit(solution)/shard_map/all_to_all | solution.py:54
  23.4 6.8 %copy-start.67 = (s32[16,8]{0,1:T(8,128)S(1)}, s32[16,8]{0,1:T(8,128)}, u32[]{:S(2)}) copy-start(s32[16,8]{0,1:T(8,128)} %param.17) | copy-start | bytes 1540
  23.4 8.4 %copy-start.68 = (s32[128]{0:T(128)S(1)}, s32[128]{0:T(128)}, u32[]{:S(2)}) copy-start(s32[128]{0:T(128)} %param.15) | copy-start | bytes 1540
  23.4 440.0 %reduce-scatter.2.cloned.1.call-start = ((), (), s32[]{:S(2)}) async-start(), calls=%async_computation.3 | async-start | bytes 2162688 | tf_op jit(solution)/shard_map/reduce_scatter | solution.py:122
  140.8 6.0 %copy-start.5 = (f32[64,8,1024]{2,1,0:T(8,128)S(1)}, f32[64,8,1024]{2,1,0:T(8,128)}, u32[]{:S(2)}) copy-start(f32[64,8,1024]{2,1,0:T(8,128)} %get-tuple-element.64) | copy-start | bytes 6291460
  161.6 5.8 %copy-start.3 = (f32[64,8,1024]{2,1,0:T(8,128)S(1)}, f32[64,8,1024]{2,1,0:T(8,128)}, u32[]{:S(2)}) copy-start(f32[64,8,1024]{2,1,0:T(8,128)} %get-tuple-element.56) | copy-start | bytes 6291460
  172.0 5.8 %copy-start.2 = (f32[64,8,1024]{2,1,0:T(8,128)S(1)}, f32[64,8,1024]{2,1,0:T(8,128)}, u32[]{:S(2)}) copy-start(f32[64,8,1024]{2,1,0:T(8,128)} %get-tuple-element.84) | copy-start | bytes 6291460
  185.0 6.1 %copy-start.54 = (f32[64,8]{1,0:T(8,128)S(1)}, f32[64,8]{1,0:T(8,128)}, u32[]{:S(2)}) copy-start(f32[64,8]{1,0:T(8,128)} %fusion.12) | copy-start | bytes 6148
  185.0 6.2 %copy-start.24 = (f32[64,8]{1,0:T(8,128)S(1)}, f32[64,8]{1,0:T(8,128)}, u32[]{:S(2)}) copy-start(f32[64,8]{1,0:T(8,128)} %copy-done.23) | copy-start | bytes 6148
  186.5 6.0 %copy-start.55 = (f32[64,8]{1,0:T(8,128)S(1)}, f32[64,8]{1,0:T(8,128)}, u32[]{:S(2)}) copy-start(f32[64,8]{1,0:T(8,128)} %fusion.10) | copy-start | bytes 6148
  186.5 6.1 %copy-start.27 = (f32[64,8]{1,0:T(8,128)S(1)}, f32[64,8]{1,0:T(8,128)}, u32[]{:S(2)}) copy-start(f32[64,8]{1,0:T(8,128)} %copy-done.26) | copy-start | bytes 6148
  186.5 7.3 %copy-start.56 = (f32[64,8]{1,0:T(8,128)S(1)}, f32[64,8]{1,0:T(8,128)}, u32[]{:S(2)}) copy-start(f32[64,8]{1,0:T(8,128)} %fusion.8) | copy-start | bytes 6148
  186.5 7.4 %copy-start.30 = (f32[64,8]{1,0:T(8,128)S(1)}, f32[64,8]{1,0:T(8,128)}, u32[]{:S(2)}) copy-start(f32[64,8]{1,0:T(8,128)} %copy-done.29) | copy-start | bytes 6148
  187.9 7.2 %copy-start.58 = (f32[64,8]{1,0:T(8,128)S(1)}, f32[64,8]{1,0:T(8,128)}, u32[]{:S(2)}) copy-start(f32[64,8]{1,0:T(8,128)} %fusion.6) | copy-start | bytes 6148
  187.9 7.3 %copy-start.33 = (f32[64,8]{1,0:T(8,128)S(1)}, f32[64,8]{1,0:T(8,128)}, u32[]{:S(2)}) copy-start(f32[64,8]{1,0:T(8,128)} %copy-done.32) | copy-start | bytes 6148
  187.9 8.6 %copy-start.59 = (f32[64,8]{1,0:T(8,128)S(1)}, f32[64,8]{1,0:T(8,128)}, u32[]{:S(2)}) copy-start(f32[64,8]{1,0:T(8,128)} %fusion.4) | copy-start | bytes 6148
  187.9 8.7 %copy-start.37 = (f32[64,8]{1,0:T(8,128)S(1)}, f32[64,8]{1,0:T(8,128)}, u32[]{:S(2)}) copy-start(f32[64,8]{1,0:T(8,128)} %copy-done.36) | copy-start | bytes 6148
  189.4 7.5 %copy-start.60 = (f32[64,8]{1,0:T(8,128)S(1)}, f32[64,8]{1,0:T(8,128)}, u32[]{:S(2)}) copy-start(f32[64,8]{1,0:T(8,128)} %fusion.2) | copy-start | bytes 6148
  189.4 7.6 %copy-start.39 = (f32[64,8]{1,0:T(8,128)S(1)}, f32[64,8]{1,0:T(8,128)}, u32[]{:S(2)}) copy-start(f32[64,8]{1,0:T(8,128)} %copy-done.38) | copy-start | bytes 6148
  189.4 8.9 %copy-start.61 = (f32[64,8]{1,0:T(8,128)S(1)}, f32[64,8]{1,0:T(8,128)}, u32[]{:S(2)}) copy-start(f32[64,8]{1,0:T(8,128)} %fusion) | copy-start | bytes 6148
  189.4 9.0 %copy-start.35 = (f32[64,8]{1,0:T(8,128)S(1)}, f32[64,8]{1,0:T(8,128)}, u32[]{:S(2)}) copy-start(f32[64,8]{1,0:T(8,128)} %copy-done.34) | copy-start | bytes 6148
  190.8 130.0 %copy-start.57 = (f32[64,8]{1,0:T(8,128)S(1)}, f32[64,8]{1,0:T(8,128)}, u32[]{:S(2)}) copy-start(f32[64,8]{1,0:T(8,128)} %fusion.14) | copy-start | bytes 6148
  (50 other events, 165.1 us)
Sparse Core Ops, SparseCore 0:
  9.8 52.2 all-gather.1
  330.1 86.2 reduce-scatter.1
where the time goes:
time: 478 us; the launch traced here: 472 us
  blocking collectives  245 us (51%)
  matrix products  68.8 us (14%)
  local copies, waits for them, and re-layouts  57.5 us (12%)
  other arithmetic  45.6 us (10%)
  waiting for transfers between devices  30.6 us (6%)
  between operations  15.2 us (3%)
  starting transfers between devices  9.19 us (2%)
    unnamed x1, blocking collectives  124 us
    pmax x1, blocking collectives, body(): peak_all = lax.pmax(peak_rows, 'ctx')  121 us
    all_gather x1, waiting for transfers between devices, body(): gathered_suffix = lax.all_gather(queries, 'ctx', axis=2, tiled=True)  29.9 us
    dot_general x8, matrix products, body(): jnp.einsum('qgd,nd->qgn', query_head, key_prompt, preferred_element_type=...  26.7 us
    reduce_sum x8, other arithmetic, body(): jnp.sum(weight_prompt, axis=2) + jnp.sum(weight_suffix, axis=2)  21.7 us
    dot_general x8, matrix products, body(): jnp.einsum('qgd,qnd->qgn', query_head, key_suffix, preferred_element_type...  19 us
    gather x8, local copies, waits for them, and re-layouts, body(): jnp.take(resident[:, :, key_start:key_start + HEAD_SIZE], first_step, axi...  18.7 us
    dot_general x8, matrix products, body(): jnp.einsum('qgn,nd->qgd', weight_prompt.astype(jnp.bfloat16), value_promp...  17.3 us
  transfers between devices with their start and end apart: 3, of which 1 were waited for; matrix products, arithmetic and copies ran while one was open for 11% of the time, Pallas kernels for 0%

commit v1 on v0

v1 whole, which is shorter than its diff:
```python
import functools
import math

import jax
import jax.numpy as jnp
from jax import lax
from jax.experimental import pallas as pl
from jax.experimental.pallas import tpu as pltpu
from jax.sharding import PartitionSpec as P

MESH = pl.DeviceIdType.MESH

QUERY_HEAD_COUNT = 64
KEY_VALUE_HEADS = 8
HEAD_SIZE = 128
DRAFT_STEPS = 4
WIDTH = KEY_VALUE_HEADS * HEAD_SIZE
REQ = 8
CTX = 32
PER_REQ = 16
CAP = 2
SPAN = 32
PROMPT = 1024
TOKENS = DRAFT_STEPS * PER_REQ
ROWS = 2 * TOKENS
OWNERS = CTX // KEY_VALUE_HEADS
STAT = 8
MASKED = -1e30
EXP_SCALE = math.log2(math.e) / math.sqrt(HEAD_SIZE)


def nt_dot(a, b):
    return lax.dot_general(a, b, (((1,), (1,)), ((), ())), preferred_element_type=jnp.float32)


def kernel(
    roots, parents, block_mask, queries_hbm, draft_hbm, prompt_hbm, suffix_hbm, out_ref,
    prompt, suffix, draft, query_in, zsend, zrecv, query_all, rsend, rrecv, mask, pick, slot,
    load_sem, zs_sem, zr_sem, qs_sem, qr_sem, rs_sem, rr_sem,
):
    z = lax.axis_index("req")
    c = lax.axis_index("ctx")
    group = c // OWNERS

    barrier = pltpu.get_barrier_semaphore()

    def greet_z(i, _):
        pl.semaphore_signal(barrier, inc=1, device_id=(lax.rem(z + i, REQ), c), device_id_type=MESH)
        return 0

    def greet_ctx(i, _):
        pl.semaphore_signal(barrier, inc=1, device_id=(z, lax.rem(c + i, CTX)), device_id_type=MESH)
        return 0

    lax.fori_loop(1, REQ, greet_z, 0)
    lax.fori_loop(1, CTX, greet_ctx, 0)

    load_suffix = pltpu.make_async_copy(suffix_hbm, suffix, load_sem.at[0])
    load_query = pltpu.make_async_copy(queries_hbm, query_in, load_sem.at[1])
    load_prompt = pltpu.make_async_copy(prompt_hbm, prompt, load_sem.at[2])
    load_draft = pltpu.make_async_copy(draft_hbm, draft, load_sem.at[3])
    load_suffix.start()
    load_query.start()
    load_prompt.start()
    load_draft.start()

    def choose(d, _):
        count, first, second = jnp.int32(0), jnp.int32(0), jnp.int32(0)
        for j in range(PER_REQ):
            root = roots[d * PER_REQ + j]
            mine = (root >> 4) == z
            local = root & 15
            first = jnp.where(mine & (count == 0), local, first)
            second = jnp.where(mine & (count == 1), local, second)
            count = count + mine.astype(jnp.int32)
        pick[2 * d] = first
        pick[2 * d + 1] = second
        return 0

    lax.fori_loop(0, REQ, choose, 0)

    load_query.wait()
    query_all[c, 0:TOKENS, :] = query_in[:, 0:HEAD_SIZE]
    query_all[c, TOKENS:ROWS, :] = query_in[:, HEAD_SIZE : 2 * HEAD_SIZE]
    load_suffix.wait()

    def head_of(k):
        return lax.rem(group + 1 + k, KEY_VALUE_HEADS)

    def pack(k):
        key_at = pl.ds(pl.multiple_of(head_of(k) * HEAD_SIZE, HEAD_SIZE), HEAD_SIZE)
        value_at = pl.ds(pl.multiple_of(WIDTH + head_of(k) * HEAD_SIZE, HEAD_SIZE), HEAD_SIZE)

        def one(d, _):
            for s in range(CAP):
                index = pick[2 * d + s]
                zsend[k, d, 0, s * SPAN : (s + 1) * SPAN, :] = suffix[index, :, key_at]
                zsend[k, d, 1, s * SPAN : (s + 1) * SPAN, :] = suffix[index, :, value_at]
            return 0

        lax.fori_loop(0, REQ, one, 0)
        zrecv[k, z] = zsend[k, z]

    def z_copy(k, i):
        d = lax.rem(z + i, REQ)
        return pltpu.make_async_remote_copy(
            src_ref=zsend.at[k, d],
            dst_ref=zrecv.at[k, z],
            send_sem=zs_sem.at[k, d],
            recv_sem=zr_sem.at[k, z],
            device_id=(d, c),
            device_id_type=MESH,
        )

    def z_arrival(k, i):
        s = lax.rem(z + i, REQ)
        return pltpu.make_async_remote_copy(
            src_ref=zsend.at[k, s],
            dst_ref=zrecv.at[k, s],
            send_sem=zs_sem.at[k, s],
            recv_sem=zr_sem.at[k, s],
            device_id=(s, c),
            device_id_type=MESH,
        )

    def q_copy(to):
        return pltpu.make_async_remote_copy(
            src_ref=query_all.at[c],
            dst_ref=query_all.at[c],
            send_sem=qs_sem.at[to],
            recv_sem=qr_sem.at[c],
            device_id=(z, to),
            device_id_type=MESH,
        )

    def q_arrival(s):
        return pltpu.make_async_remote_copy(
            src_ref=query_all.at[s],
            dst_ref=query_all.at[s],
            send_sem=qs_sem.at[s],
            recv_sem=qr_sem.at[s],
            device_id=(z, s),
            device_id_type=MESH,
        )

    def r_copy(to):
        return pltpu.make_async_remote_copy(
            src_ref=rsend.at[to],
            dst_ref=rrecv.at[c],
            send_sem=rs_sem.at[to],
            recv_sem=rr_sem.at[c],
            device_id=(z, to),
            device_id_type=MESH,
        )

    def r_arrival(s):
        return pltpu.make_async_remote_copy(
            src_ref=rsend.at[s],
            dst_ref=rrecv.at[s],
            send_sem=rs_sem.at[s],
            recv_sem=rr_sem.at[s],
            device_id=(z, s),
            device_id_type=MESH,
        )

    def send_stage(k):
        for i in (4, 3, 5, 2, 6, 1, 7):
            z_copy(k, i).start()

    pack(0)
    pl.semaphore_wait(barrier, REQ - 1 + CTX - 1)
    send_stage(0)

    def send_query(i, _):
        to = lax.rem(group + 2 * KEY_VALUE_HEADS - 1 - i // OWNERS, KEY_VALUE_HEADS) * OWNERS + lax.rem(c + i, OWNERS)

        @pl.when(to != c)
        def _():
            q_copy(to).start()

        return 0

    lax.fori_loop(0, CTX, send_query, 0)

    def pack_and_send(k, _):
        pack(k)
        send_stage(k)
        return 0

    lax.fori_loop(1, KEY_VALUE_HEADS, pack_and_send, 0)

    own = [roots[z * PER_REQ + j] >> 4 for j in range(PER_REQ)]
    for j in range(PER_REQ):
        rank = jnp.int32(0)
        for i in range(j):
            rank = rank + (own[i] == own[j]).astype(jnp.int32)
        slot[j] = own[j] * CAP + rank

    lane_slot = lax.broadcasted_iota(jnp.int32, (1, REQ * CAP * SPAN), 1) // SPAN
    lane_token = lax.rem(lax.broadcasted_iota(jnp.int32, (1, ROWS), 1), TOKENS)

    def trace(j, carry):
        lines = list(carry)
        for t in range(DRAFT_STEPS):
            at = j
            path = {t: at}
            for back in range(t - 1, -1, -1):
                at = parents[back, at]
                path[back] = at
            here = jnp.where(block_mask[at, group] > 0, slot[at], -1)
            mask[pl.ds(t * PER_REQ + j, 1), :] = jnp.where(lane_slot == here, 0.0, MASKED)
            for s in range(t + 1):
                lines[s] = jnp.where(lane_token == t * PER_REQ + j, path[s], lines[s])
        return tuple(lines)

    lines = lax.fori_loop(
        0, PER_REQ, trace, tuple(jnp.full((1, ROWS), -1, jnp.int32) for _ in range(DRAFT_STEPS))
    )

    load_prompt.wait()
    load_draft.wait()
    lane = lax.broadcasted_iota(jnp.int32, (ROWS, HEAD_SIZE), 1)

    def stage(k, _):
        h = head_of(k)
        key_at = pl.ds(pl.multiple_of(h * HEAD_SIZE, HEAD_SIZE), HEAD_SIZE)
        value_at = pl.ds(pl.multiple_of(WIDTH + h * HEAD_SIZE, HEAD_SIZE), HEAD_SIZE)

        def wait_z(i, _):
            z_arrival(k, i).wait_recv()
            return 0

        lax.fori_loop(1, REQ, wait_z, 0)

        def chunk(part, _):
            owner = h * OWNERS + part

            @pl.when(owner != c)
            def _():
                q_arrival(owner).wait_recv()

            rows = query_all[owner]
            score_prompt = nt_dot(rows, prompt[:, key_at])
            keys = zrecv[k, :, 0].reshape(REQ * CAP * SPAN, HEAD_SIZE)
            values = zrecv[k, :, 1].reshape(REQ * CAP * SPAN, HEAD_SIZE)
            bias = mask[...]
            score_suffix = nt_dot(rows, keys) + jnp.concatenate([bias, bias], axis=0)
            peak = jnp.maximum(
                jnp.max(score_prompt, axis=1, keepdims=True), jnp.max(score_suffix, axis=1, keepdims=True)
            )
            weight_prompt = jnp.exp2((score_prompt - peak) * EXP_SCALE)
            weight_suffix = jnp.exp2((score_suffix - peak) * EXP_SCALE)
            total = jnp.sum(weight_prompt, axis=1, keepdims=True) + jnp.sum(weight_suffix, axis=1, keepdims=True)
            accum = jnp.dot(
                weight_prompt.astype(jnp.bfloat16), prompt[:, value_at], preferred_element_type=jnp.float32
            )
            accum = accum + jnp.dot(weight_suffix.astype(jnp.bfloat16), values, preferred_element_type=jnp.float32)
            rsend[owner, 0:ROWS, :] = accum
            stats = jnp.transpose(jnp.where(lane == 0, peak, total))
            rsend[owner, ROWS : ROWS + STAT, :] = stats[0:STAT]

            @pl.when(owner != c)
            def _():
                r_copy(owner).start()

            return 0

        lax.fori_loop(0, OWNERS, chunk, 0)
        return 0

    lax.fori_loop(0, KEY_VALUE_HEADS, stage, 0)

    rrecv[c] = rsend[c]

    key_at = pl.ds(pl.multiple_of(group * HEAD_SIZE, HEAD_SIZE), HEAD_SIZE)
    value_at = pl.ds(pl.multiple_of(WIDTH + group * HEAD_SIZE, HEAD_SIZE), HEAD_SIZE)
    score_draft = nt_dot(draft[:, key_at], query_all[c])
    particle = lax.broadcasted_iota(jnp.int32, (PER_REQ, ROWS), 0)
    allowed = jnp.concatenate([jnp.where(particle == line, 1, 0) for line in lines], axis=0)
    score_draft = jnp.where(allowed > 0, score_draft, MASKED)

    def wait_r(i, _):
        r_arrival(lax.rem(c + i, CTX)).wait_recv()
        return 0

    lax.fori_loop(1, CTX, wait_r, 0)

    peaks = rrecv[:, ROWS, :]
    totals = rrecv[:, ROWS + 1, :]
    highest = jnp.maximum(jnp.max(peaks, axis=0, keepdims=True), jnp.max(score_draft, axis=0, keepdims=True))
    factor = jnp.exp2((peaks - highest) * EXP_SCALE)
    weight_draft = jnp.exp2((score_draft - highest) * EXP_SCALE)
    total = jnp.sum(totals * factor, axis=0, keepdims=True) + jnp.sum(weight_draft, axis=0, keepdims=True)
    turned = jnp.transpose(
        jnp.concatenate([factor, jnp.broadcast_to(total, (CTX, ROWS)), weight_draft], axis=0)
    )
    numerator = jnp.dot(
        turned[:, 2 * CTX :].astype(jnp.bfloat16), draft[:, value_at], preferred_element_type=jnp.float32
    )
    for s in range(CTX):
        numerator = numerator + rrecv[s, 0:ROWS, :] * turned[:, s : s + 1]
    result = (numerator / turned[:, CTX : CTX + 1]).astype(jnp.bfloat16)
    out_ref[:, 0:HEAD_SIZE] = result[0:TOKENS]
    out_ref[:, HEAD_SIZE : 2 * HEAD_SIZE] = result[TOKENS:ROWS]

    def drain_z(k, _):
        def one(i, _):
            z_copy(k, i).wait_send()
            return 0

        return lax.fori_loop(1, REQ, one, 0)

    lax.fori_loop(0, KEY_VALUE_HEADS, drain_z, 0)

    def drain_ctx(i, _):
        to = lax.rem(c + i, CTX)
        q_copy(to).wait_send()
        r_copy(to).wait_send()
        return 0

    lax.fori_loop(1, CTX, drain_ctx, 0)


def body(prompt_key_value, suffix_key_value, roots, parents, block_mask, queries, draft_kv):
    smem = pl.BlockSpec(memory_space=pltpu.SMEM)
    anywhere = pl.BlockSpec(memory_space=pl.ANY)
    bf16, f32 = jnp.bfloat16, jnp.float32
    result = pl.pallas_call(
        kernel,
        out_shape=jax.ShapeDtypeStruct((TOKENS, 2 * HEAD_SIZE), bf16),
        in_specs=[smem, smem, smem, anywhere, anywhere, anywhere, anywhere],
        out_specs=pl.BlockSpec(memory_space=pltpu.VMEM),
        scratch_shapes=[
            pltpu.VMEM((PROMPT, 2 * WIDTH), bf16),
            pltpu.VMEM((PER_REQ, SPAN, 2 * WIDTH), bf16),
            pltpu.VMEM((TOKENS, 2 * WIDTH), bf16),
            pltpu.VMEM((TOKENS, 2 * HEAD_SIZE), bf16),
            pltpu.VMEM((KEY_VALUE_HEADS, REQ, 2, CAP * SPAN, HEAD_SIZE), bf16),
            pltpu.VMEM((KEY_VALUE_HEADS, REQ, 2, CAP * SPAN, HEAD_SIZE), bf16),
            pltpu.VMEM((CTX, ROWS, HEAD_SIZE), bf16),
            pltpu.VMEM((CTX, ROWS + STAT, HEAD_SIZE), f32),
            pltpu.VMEM((CTX, ROWS + STAT, HEAD_SIZE), f32),
            pltpu.VMEM((TOKENS, REQ * CAP * SPAN), f32),
            pltpu.SMEM((REQ * CAP,), jnp.int32),
            pltpu.SMEM((PER_REQ,), jnp.int32),
            pltpu.SemaphoreType.DMA((4,)),
            pltpu.SemaphoreType.DMA((KEY_VALUE_HEADS, REQ)),
            pltpu.SemaphoreType.DMA((KEY_VALUE_HEADS, REQ)),
            pltpu.SemaphoreType.DMA((CTX,)),
            pltpu.SemaphoreType.DMA((CTX,)),
            pltpu.SemaphoreType.DMA((CTX,)),
            pltpu.SemaphoreType.DMA((CTX,)),
        ],
        compiler_params=pltpu.CompilerParams(
            collective_id=0, has_side_effects=True, vmem_limit_bytes=48 * 1024 * 1024
        ),
        cost_estimate=pl.CostEstimate(flops=3_300_000_000, bytes_accessed=7_000_000, transcendentals=6_300_000),
    )(
        roots,
        parents,
        block_mask,
        queries.reshape(TOKENS, 2 * HEAD_SIZE),
        draft_kv.reshape(TOKENS, 2 * WIDTH),
        prompt_key_value,
        suffix_key_value,
    )
    return result.reshape(DRAFT_STEPS, PER_REQ, 2 * HEAD_SIZE)


def solution(mesh):
    return jax.shard_map(
        body,
        mesh=mesh,
        in_specs=(
            P("ctx", None),
            P("req", "ctx", None),
            P(),
            P(None, "req"),
            P("req", None),
            P(None, "req", "ctx"),
            P(None, "req", None),
        ),
        out_specs=P(None, "req", "ctx"),
        check_vma=False,
    )
```

time: 478 us -> 76.4 us (0.16); the launches traced: 472 us -> 76.2 us
  blocking collectives: 245 us -> 0 us
  Pallas kernels: 0 us -> 70.2 us
  matrix products: 68.8 us -> 0 us
  local copies, waits for them, and re-layouts: 57.5 us -> 6.01 us
  other arithmetic: 45.6 us -> 0 us
  waiting for transfers between devices: 30.6 us -> 0 us
  between operations: 15.2 us -> 0.01 us
  starting transfers between devices: 9.19 us -> 0 us
    unnamed x1 -> x0, blocking collectives: 124 us -> none
    pmax x1 -> x0, blocking collectives: 121 us -> none  [body(): peak_all = lax.pmax(peak_rows, 'ctx')]
    pallas_call x0 -> x1, Pallas kernels: none -> 70.2 us  [body(): pl.pallas_call(kernel, out_shape=jax.ShapeDtypeStruct((TOKENS, 2 * HEAD_S...]
    dot_general x34 -> x0, matrix products: 68.8 us -> none  [the longest x8 26.7 us: body(): jnp.einsum('qgd,nd->qgn', query_head, key_prompt, preferred_element_type=...]
    gather x29 -> x0, local copies, waits for them, and re-layouts: 45.2 us -> none  [the longest x8 18.7 us: body(): jnp.take(resident[:, :, key_start:key_start + HEAD_SIZE], first_step, axi...]
    all_gather x1 -> x0, waiting for transfers between devices: 29.9 us -> none  [body(): gathered_suffix = lax.all_gather(queries, 'ctx', axis=2, tiled=True)]
    reduce_sum x19 -> x0, other arithmetic: 29.6 us -> none  [the longest x8 21.7 us: body(): jnp.sum(weight_prompt, axis=2) + jnp.sum(weight_suffix, axis=2)]
    all_to_all x1 -> x0, starting transfers between devices: 9.15 us -> none  [body(): lax.all_to_all(outgoing, 'req', split_axis=0, concat_axis=0, tiled=True)]
  transfers between devices with their start and end apart: 3 -> 0, of which waited for: 1 -> 0; matrix products, arithmetic and copies ran while one was open for 11% -> 0% of each run, Pallas kernels for 0% -> 0%
where the time goes in v1:
time: 76.4 us; the launch traced here: 76.2 us
  Pallas kernels  70.2 us (92%)
  local copies, waits for them, and re-layouts  6.01 us (8%)
    pallas_call x1, Pallas kernels, body(): pl.pallas_call(kernel, out_shape=jax.ShapeDtypeStruct((TOKENS, 2 * HEAD_S...  70.2 us
    unnamed x12, local copies, waits for them, and re-layouts  6.01 us

profile of v1, /device:TPU:1, one launch (start us, length us, event | category | flops | bytes accessed | tf_op | source)
XLA Modules:
  0.0 76.2 jit_solution(6174970122134816588)
XLA Ops:
  0.0 0.8 copy.8.block_mask
  0.8 0.0 copy-start
  0.8 1.6 %copy-done = bf16[16,32,2048]{2,1,0:T(8,128)(2,1)S(1)} copy-done((bf16[16,32,2048]{2,1,0:T(8,128)(2,1)S(1)}, bf16[16,32,2048]{2,1,0:T(8,128)(2,1)}, u32[]{:S(2)}) %copy-start) | copy-done | bytes 2097176
  2.3 0.0 copy-start.1
  2.4 0.9 %copy-done.1 = bf16[4,16,2048]{2,1,0:T(8,128)(2,1)S(1)} copy-done((bf16[4,16,2048]{2,1,0:T(8,128)(2,1)S(1)}, bf16[4,16,2048]{2,1,0:T(8,128)(2,1)}, u32[]{:S(2)}) %copy-start.1) | copy-done | bytes 262168
  3.3 0.0 copy-start.2
  3.3 0.8 copy-done.2
  4.1 0.0 copy-start.3
  4.1 0.7 copy-done.3
  4.7 0.0 copy-start.4
  4.7 0.7 copy-done.4
  5.4 70.2 %shard_map.73 = bf16[64,256]{1,0:T(8,128)(2,1)S(1)} custom-call(s32[128]{0:T(128)S(1)} %copy-done.4, s32[3,16]{1,0:T(4,128)S(1)} %copy-done.3, s32[16,8]{1,0:T(8,128)S(1)} %copy.8.block_mask, bf16[64,256]{1,0:T(8,128)(2,1)S(1)} %bitcast.5, bf16[64,2048]{1,0:T(8,128)(2,1)S(1)} %bitcast.4, bf16[1024,2048]{1,0:T(8,128)(2,1)} %prompt_hbm.1, ...), custom_call_target="tpu_custom_call" | custom-call | flops 3300000000 | bytes 7000000 | tf_op jit(solution)/shard_map/pallas_call | solution.py:328
  75.6 0.6 copy.10
Async XLA Ops:
  0.8 1.6 %copy-start = (bf16[16,32,2048]{2,1,0:T(8,128)(2,1)S(1)}, bf16[16,32,2048]{2,1,0:T(8,128)(2,1)}, u32[]{:S(2)}) copy-start(bf16[16,32,2048]{2,1,0:T(8,128)(2,1)} %suffix_hbm.1) | copy-start | bytes 6291460
  2.3 0.9 %copy-start.1 = (bf16[4,16,2048]{2,1,0:T(8,128)(2,1)S(1)}, bf16[4,16,2048]{2,1,0:T(8,128)(2,1)}, u32[]{:S(2)}) copy-start(bf16[4,16,2048]{2,1,0:T(8,128)(2,1)} %param.13) | copy-start | bytes 786436
  3.3 0.8 copy-start.2
  4.1 0.7 copy-start.3
  4.7 0.7 copy-start.4

commit v2 on v1

v2 whole, which is shorter than its diff:
```python
import functools
import math

import jax
import jax.numpy as jnp
from jax import lax
from jax.experimental import pallas as pl
from jax.experimental.pallas import tpu as pltpu
from jax.sharding import PartitionSpec as P

MESH = pl.DeviceIdType.MESH

QUERY_HEAD_COUNT = 64
KEY_VALUE_HEADS = 8
HEAD_SIZE = 128
DRAFT_STEPS = 4
WIDTH = KEY_VALUE_HEADS * HEAD_SIZE
REQ = 8
CTX = 32
CHIPS = CTX // 2
PER_REQ = 16
CAP = 2
SPAN = 32
PROMPT = 1024
TOKENS = DRAFT_STEPS * PER_REQ
ROWS = 2 * TOKENS
OWNERS = CTX // KEY_VALUE_HEADS
STAT = 8
MASKED = -1e30
EXP_SCALE = math.log2(math.e) / math.sqrt(HEAD_SIZE)


def nt_dot(a, b):
    return lax.dot_general(a, b, (((1,), (1,)), ((), ())), preferred_element_type=jnp.float32)


def kernel(
    roots_hbm, parents_hbm, mask_hbm, queries_hbm, draft_hbm, prompt_hbm, suffix_hbm, out_ref,
    prompt, suffix, draft, query_in, zsend, zrecv, query_all, xsend, xrecv, keep, rsend, rrecv, mask,
    roots, parents, block_mask, pick, slot,
    load_sem, zs_sem, zr_sem, qs_sem, qf_sem, qr_sem, xs_sem, xr_sem, rs_sem, rr_sem,
):
    z = lax.axis_index("req")
    c = lax.axis_index("ctx")
    group = c // OWNERS
    chip = c // 2
    core = lax.rem(c, 2)
    sibling = chip * 2 + 1 - core

    barrier = pltpu.get_barrier_semaphore()

    def greet_z(i, _):
        pl.semaphore_signal(barrier, inc=1, device_id=(lax.rem(z + i, REQ), c), device_id_type=MESH)
        return 0

    def greet_chip(i, _):
        to = lax.rem(chip + i, CHIPS) * 2 + core
        pl.semaphore_signal(barrier, inc=1, device_id=(z, to), device_id_type=MESH)
        return 0

    lax.fori_loop(1, REQ, greet_z, 0)
    lax.fori_loop(1, CHIPS, greet_chip, 0)
    pl.semaphore_signal(barrier, inc=1, device_id=(z, sibling), device_id_type=MESH)

    load_suffix = pltpu.make_async_copy(suffix_hbm, suffix, load_sem.at[0])
    load_query = pltpu.make_async_copy(queries_hbm, query_in, load_sem.at[1])
    load_prompt = pltpu.make_async_copy(prompt_hbm, prompt, load_sem.at[2])
    load_draft = pltpu.make_async_copy(draft_hbm, draft, load_sem.at[3])
    load_roots = pltpu.make_async_copy(roots_hbm, roots, load_sem.at[4])
    load_parents = pltpu.make_async_copy(parents_hbm, parents, load_sem.at[5])
    load_mask = pltpu.make_async_copy(mask_hbm, block_mask, load_sem.at[6])
    load_roots.start()
    load_suffix.start()
    load_query.start()
    load_parents.start()
    load_mask.start()
    load_prompt.start()
    load_draft.start()

    def choose(d, _):
        count, first, second = jnp.int32(0), jnp.int32(0), jnp.int32(0)
        for j in range(PER_REQ):
            root = roots[d * PER_REQ + j]
            mine = (root >> 4) == z
            local = root & 15
            first = jnp.where(mine & (count == 0), local, first)
            second = jnp.where(mine & (count == 1), local, second)
            count = count + mine.astype(jnp.int32)
        pick[2 * d] = first
        pick[2 * d + 1] = second
        return 0

    load_roots.wait()
    lax.fori_loop(0, REQ, choose, 0)

    load_query.wait()
    query_all[c, 0:TOKENS, :] = query_in[:, 0:HEAD_SIZE]
    query_all[c, TOKENS:ROWS, :] = query_in[:, HEAD_SIZE : 2 * HEAD_SIZE]
    load_suffix.wait()

    def head_of(k):
        return lax.rem(group + 1 + k, KEY_VALUE_HEADS)

    def pack(k):
        key_at = pl.ds(pl.multiple_of(head_of(k) * HEAD_SIZE, HEAD_SIZE), HEAD_SIZE)
        value_at = pl.ds(pl.multiple_of(WIDTH + head_of(k) * HEAD_SIZE, HEAD_SIZE), HEAD_SIZE)

        def one(d, _):
            for s in range(CAP):
                index = pick[2 * d + s]
                zsend[k, d, 0, s * SPAN : (s + 1) * SPAN, :] = suffix[index, :, key_at]
                zsend[k, d, 1, s * SPAN : (s + 1) * SPAN, :] = suffix[index, :, value_at]
            return 0

        lax.fori_loop(0, REQ, one, 0)
        zrecv[k, z] = zsend[k, z]

    def z_copy(k, i):
        d = lax.rem(z + i, REQ)
        return pltpu.make_async_remote_copy(
            src_ref=zsend.at[k, d],
            dst_ref=zrecv.at[k, z],
            send_sem=zs_sem.at[k, d],
            recv_sem=zr_sem.at[k, z],
            device_id=(d, c),
            device_id_type=MESH,
        )

    def z_arrival(k, i):
        s = lax.rem(z + i, REQ)
        return pltpu.make_async_remote_copy(
            src_ref=zsend.at[k, s],
            dst_ref=zrecv.at[k, s],
            send_sem=zs_sem.at[k, s],
            recv_sem=zr_sem.at[k, s],
            device_id=(s, c),
            device_id_type=MESH,
        )

    def q_send(source, to, sem):
        return pltpu.make_async_remote_copy(
            src_ref=query_all.at[source],
            dst_ref=query_all.at[source],
            send_sem=sem,
            recv_sem=qr_sem.at[source],
            device_id=(z, to),
            device_id_type=MESH,
        )

    def q_copy(to):
        return q_send(c, to, qs_sem.at[to])

    def q_forward(source):
        return q_send(source, sibling, qf_sem.at[source])

    def x_copy(k, half):
        return pltpu.make_async_remote_copy(
            src_ref=xsend.at[k, half],
            dst_ref=xrecv.at[k, half],
            send_sem=xs_sem.at[k, half],
            recv_sem=xr_sem.at[k, half],
            device_id=(z, sibling),
            device_id_type=MESH,
        )

    def r_copy(to_chip):
        return pltpu.make_async_remote_copy(
            src_ref=rsend.at[to_chip],
            dst_ref=rrecv.at[chip],
            send_sem=rs_sem.at[to_chip],
            recv_sem=rr_sem.at[chip],
            device_id=(z, to_chip * 2 + core),
            device_id_type=MESH,
        )

    def r_arrival(from_chip):
        return pltpu.make_async_remote_copy(
            src_ref=rsend.at[from_chip],
            dst_ref=rrecv.at[from_chip],
            send_sem=rs_sem.at[from_chip],
            recv_sem=rr_sem.at[from_chip],
            device_id=(z, from_chip * 2 + core),
            device_id_type=MESH,
        )

    def send_stage(k):
        for i in (4, 3, 5, 2, 6, 1, 7):
            z_copy(k, i).start()

    pack(0)
    pl.semaphore_wait(barrier, REQ - 1 + CHIPS)
    send_stage(0)

    q_copy(sibling).start()

    def send_query(i, _):
        to = lax.rem(group + 2 * KEY_VALUE_HEADS - 1 - i // 2, KEY_VALUE_HEADS) * 2 + lax.rem(chip + i, 2)

        @pl.when(to != chip)
        def _():
            q_copy(to * 2 + core).start()

        return 0

    lax.fori_loop(0, CHIPS, send_query, 0)

    def pack_and_send(k, _):
        pack(k)
        send_stage(k)
        return 0

    lax.fori_loop(1, KEY_VALUE_HEADS, pack_and_send, 0)

    load_parents.wait()
    load_mask.wait()

    own = [roots[z * PER_REQ + j] >> 4 for j in range(PER_REQ)]
    for j in range(PER_REQ):
        rank = jnp.int32(0)
        for i in range(j):
            rank = rank + (own[i] == own[j]).astype(jnp.int32)
        slot[j] = own[j] * CAP + rank

    lane_slot = lax.broadcasted_iota(jnp.int32, (1, REQ * CAP * SPAN), 1) // SPAN
    lane_token = lax.rem(lax.broadcasted_iota(jnp.int32, (1, ROWS), 1), TOKENS)

    def trace(j, carry):
        lines = list(carry)
        for t in range(DRAFT_STEPS):
            at = j
            path = {t: at}
            for back in range(t - 1, -1, -1):
                at = parents[back, at]
                path[back] = at
            here = jnp.where(block_mask[group, at] > 0, slot[at], -1)
            mask[pl.ds(t * PER_REQ + j, 1), :] = jnp.where(lane_slot == here, 0.0, MASKED)
            for s in range(t + 1):
                lines[s] = jnp.where(lane_token == t * PER_REQ + j, path[s], lines[s])
        return tuple(lines)

    lines = lax.fori_loop(
        0, PER_REQ, trace, tuple(jnp.full((1, ROWS), -1, jnp.int32) for _ in range(DRAFT_STEPS))
    )

    load_prompt.wait()
    load_draft.wait()
    lane = lax.broadcasted_iota(jnp.int32, (ROWS, HEAD_SIZE), 1)

    def hand_on(k):
        for half in range(2):
            owner = head_of(k) * OWNERS + core + 2 * half

            @pl.when(owner != c)
            def _():
                q_send(owner, sibling, qf_sem.at[owner]).wait_recv()
                q_forward(owner).start()

    def partial(k, owner):
        h = head_of(k)
        key_at = pl.ds(pl.multiple_of(h * HEAD_SIZE, HEAD_SIZE), HEAD_SIZE)
        value_at = pl.ds(pl.multiple_of(WIDTH + h * HEAD_SIZE, HEAD_SIZE), HEAD_SIZE)
        rows = query_all[owner]
        score_prompt = nt_dot(rows, prompt[:, key_at])
        keys = zrecv[k, :, 0].reshape(REQ * CAP * SPAN, HEAD_SIZE)
        values = zrecv[k, :, 1].reshape(REQ * CAP * SPAN, HEAD_SIZE)
        bias = mask[...]
        score_suffix = nt_dot(rows, keys) + jnp.concatenate([bias, bias], axis=0)
        peak = jnp.maximum(
            jnp.max(score_prompt, axis=1, keepdims=True), jnp.max(score_suffix, axis=1, keepdims=True)
        )
        weight_prompt = jnp.exp2((score_prompt - peak) * EXP_SCALE)
        weight_suffix = jnp.exp2((score_suffix - peak) * EXP_SCALE)
        total = jnp.sum(weight_prompt, axis=1, keepdims=True) + jnp.sum(weight_suffix, axis=1, keepdims=True)
        accum = jnp.dot(
            weight_prompt.astype(jnp.bfloat16), prompt[:, value_at], preferred_element_type=jnp.float32
        )
        accum = accum + jnp.dot(weight_suffix.astype(jnp.bfloat16), values, preferred_element_type=jnp.float32)
        return accum, jnp.where(lane == 0, peak, total)

    def stage(k, _):
        @pl.when(k < KEY_VALUE_HEADS - 1)
        def _():
            hand_on(k + 1)

        def wait_z(i, _):
            z_arrival(k, i).wait_recv()
            return 0

        lax.fori_loop(1, REQ, wait_z, 0)

        def give(half, _):
            owner = head_of(k) * OWNERS + 1 - core + 2 * half
            q_send(owner, sibling, qf_sem.at[owner]).wait_recv()
            accum, stats = partial(k, owner)
            xsend[k, half, 0:ROWS, :] = accum
            xsend[k, half, ROWS : 2 * ROWS, :] = stats
            x_copy(k, half).start()
            return 0

        lax.fori_loop(0, 2, give, 0)

        def hold(half, _):
            accum, stats = partial(k, head_of(k) * OWNERS + core + 2 * half)
            keep[half, 0:ROWS, :] = accum
            keep[half, ROWS : 2 * ROWS, :] = stats
            return 0

        lax.fori_loop(0, 2, hold, 0)

        def combine(half, _):
            to_chip = head_of(k) * 2 + half
            x_copy(k, half).wait_recv()
            peak_here, peak_there = keep[half, ROWS : 2 * ROWS, 0:1], xrecv[k, half, ROWS : 2 * ROWS, 0:1]
            total_here, total_there = keep[half, ROWS : 2 * ROWS, 1:2], xrecv[k, half, ROWS : 2 * ROWS, 1:2]
            peak = jnp.maximum(peak_here, peak_there)
            here = jnp.exp2((peak_here - peak) * EXP_SCALE)
            there = jnp.exp2((peak_there - peak) * EXP_SCALE)
            rsend[to_chip, 0:ROWS, :] = keep[half, 0:ROWS, :] * here + xrecv[k, half, 0:ROWS, :] * there
            stats = jnp.transpose(jnp.where(lane == 0, peak, total_here * here + total_there * there))
            rsend[to_chip, ROWS : ROWS + STAT, :] = stats[0:STAT]

            @pl.when(to_chip != chip)
            def _():
                r_copy(to_chip).start()

            return 0

        lax.fori_loop(0, 2, combine, 0)
        return 0

    hand_on(0)
    lax.fori_loop(0, KEY_VALUE_HEADS, stage, 0)

    rrecv[chip] = rsend[chip]

    key_at = pl.ds(pl.multiple_of(group * HEAD_SIZE, HEAD_SIZE), HEAD_SIZE)
    value_at = pl.ds(pl.multiple_of(WIDTH + group * HEAD_SIZE, HEAD_SIZE), HEAD_SIZE)
    score_draft = nt_dot(draft[:, key_at], query_all[c])
    particle = lax.broadcasted_iota(jnp.int32, (PER_REQ, ROWS), 0)
    allowed = jnp.concatenate([jnp.where(particle == line, 1, 0) for line in lines], axis=0)
    score_draft = jnp.where(allowed > 0, score_draft, MASKED)

    def wait_r(i, _):
        r_arrival(lax.rem(chip + i, CHIPS)).wait_recv()
        return 0

    lax.fori_loop(1, CHIPS, wait_r, 0)

    peaks = rrecv[:, ROWS, :]
    totals = rrecv[:, ROWS + 1, :]
    highest = jnp.maximum(jnp.max(peaks, axis=0, keepdims=True), jnp.max(score_draft, axis=0, keepdims=True))
    factor = jnp.exp2((peaks - highest) * EXP_SCALE)
    weight_draft = jnp.exp2((score_draft - highest) * EXP_SCALE)
    total = jnp.sum(totals * factor, axis=0, keepdims=True) + jnp.sum(weight_draft, axis=0, keepdims=True)
    turned = jnp.transpose(
        jnp.concatenate([factor, jnp.broadcast_to(total, (TOKENS - CHIPS, ROWS)), weight_draft], axis=0)
    )
    numerator = jnp.dot(
        turned[:, TOKENS:].astype(jnp.bfloat16), draft[:, value_at], preferred_element_type=jnp.float32
    )
    for s in range(CHIPS):
        numerator = numerator + rrecv[s, 0:ROWS, :] * turned[:, s : s + 1]
    result = (numerator / turned[:, CHIPS : CHIPS + 1]).astype(jnp.bfloat16)
    out_ref[:, 0:HEAD_SIZE] = result[0:TOKENS]
    out_ref[:, HEAD_SIZE : 2 * HEAD_SIZE] = result[TOKENS:ROWS]

    def drain_z(k, _):
        def one(i, _):
            z_copy(k, i).wait_send()
            return 0

        return lax.fori_loop(1, REQ, one, 0)

    lax.fori_loop(0, KEY_VALUE_HEADS, drain_z, 0)

    def drain_chip(i, _):
        to = lax.rem(chip + i, CHIPS)
        q_copy(to * 2 + core).wait_send()
        q_forward(to * 2 + core).wait_send()
        r_copy(to).wait_send()
        return 0

    lax.fori_loop(1, CHIPS, drain_chip, 0)
    q_copy(sibling).wait_send()

    def drain_x(k, _):
        for half in range(2):
            x_copy(k, half).wait_send()
        return 0

    lax.fori_loop(0, KEY_VALUE_HEADS, drain_x, 0)


def body(prompt_key_value, suffix_key_value, roots, parents, block_mask, queries, draft_kv):
    hbm = pl.BlockSpec(memory_space=pltpu.HBM)
    bf16, f32 = jnp.bfloat16, jnp.float32
    result = pl.pallas_call(
        kernel,
        out_shape=jax.ShapeDtypeStruct((TOKENS, 2 * HEAD_SIZE), bf16),
        in_specs=[hbm] * 7,
        out_specs=pl.BlockSpec(memory_space=pltpu.VMEM),
        scratch_shapes=[
            pltpu.VMEM((PROMPT, 2 * WIDTH), bf16),
            pltpu.VMEM((PER_REQ, SPAN, 2 * WIDTH), bf16),
            pltpu.VMEM((TOKENS, 2 * WIDTH), bf16),
            pltpu.VMEM((TOKENS, 2 * HEAD_SIZE), bf16),
            pltpu.VMEM((KEY_VALUE_HEADS, REQ, 2, CAP * SPAN, HEAD_SIZE), bf16),
            pltpu.VMEM((KEY_VALUE_HEADS, REQ, 2, CAP * SPAN, HEAD_SIZE), bf16),
            pltpu.VMEM((CTX, ROWS, HEAD_SIZE), bf16),
            pltpu.VMEM((KEY_VALUE_HEADS, 2, 2 * ROWS, HEAD_SIZE), f32),
            pltpu.VMEM((KEY_VALUE_HEADS, 2, 2 * ROWS, HEAD_SIZE), f32),
            pltpu.VMEM((2, 2 * ROWS, HEAD_SIZE), f32),
            pltpu.VMEM((CHIPS, ROWS + STAT, HEAD_SIZE), f32),
            pltpu.VMEM((CHIPS, ROWS + STAT, HEAD_SIZE), f32),
            pltpu.VMEM((TOKENS, REQ * CAP * SPAN), f32),
            pltpu.SMEM((REQ * PER_REQ,), jnp.int32),
            pltpu.SMEM((DRAFT_STEPS - 1, PER_REQ), jnp.int32),
            pltpu.SMEM((KEY_VALUE_HEADS, PER_REQ), jnp.int32),
            pltpu.SMEM((REQ * CAP,), jnp.int32),
            pltpu.SMEM((PER_REQ,), jnp.int32),
            pltpu.SemaphoreType.DMA((7,)),
            pltpu.SemaphoreType.DMA((KEY_VALUE_HEADS, REQ)),
            pltpu.SemaphoreType.DMA((KEY_VALUE_HEADS, REQ)),
            pltpu.SemaphoreType.DMA((CTX,)),
            pltpu.SemaphoreType.DMA((CTX,)),
            pltpu.SemaphoreType.DMA((CTX,)),
            pltpu.SemaphoreType.DMA((KEY_VALUE_HEADS, 2)),
            pltpu.SemaphoreType.DMA((KEY_VALUE_HEADS, 2)),
            pltpu.SemaphoreType.DMA((CHIPS,)),
            pltpu.SemaphoreType.DMA((CHIPS,)),
        ],
        compiler_params=pltpu.CompilerParams(
            collective_id=0, has_side_effects=True, vmem_limit_bytes=48 * 1024 * 1024
        ),
        cost_estimate=pl.CostEstimate(flops=3_300_000_000, bytes_accessed=7_000_000, transcendentals=6_300_000),
    )(*(
        pltpu.with_memory_space_constraint(operand, pltpu.HBM)
        for operand in (
            roots,
            parents,
            block_mask.T,
            queries.reshape(TOKENS, 2 * HEAD_SIZE),
            draft_kv.reshape(TOKENS, 2 * WIDTH),
            prompt_key_value,
            suffix_key_value,
        )
    ))
    return result.reshape(DRAFT_STEPS, PER_REQ, 2 * HEAD_SIZE)


def solution(mesh):
    return jax.shard_map(
        body,
        mesh=mesh,
        in_specs=(
            P("ctx", None),
            P("req", "ctx", None),
            P(),
            P(None, "req"),
            P("req", None),
            P(None, "req", "ctx"),
            P(None, "req", None),
        ),
        out_specs=P(None, "req", "ctx"),
        check_vma=False,
    )
```

time: 76.4 us -> 67.9 us (0.89)
  local copies, waits for them, and re-layouts: 6.01 us -> 0.62 us
  Pallas kernels: 70.2 us -> 66.7 us
    unnamed x12 -> x1, local copies, waits for them, and re-layouts: 6.01 us -> 0.62 us
    pallas_call x1, Pallas kernels: 70.2 us -> 66.7 us  [body(): pl.pallas_call(kernel, out_shape=jax.ShapeDtypeStruct((TOKENS, 2 * HEAD_S...]
where the time goes in v2:
time: 67.9 us; the launch traced here: 67.3 us
  Pallas kernels  66.7 us (98%)
    pallas_call x1, Pallas kernels, body(): pl.pallas_call(kernel, out_shape=jax.ShapeDtypeStruct((TOKENS, 2 * HEAD_S...  66.7 us

profile of v2, /device:TPU:1, one launch (start us, length us, event | category | flops | bytes accessed | tf_op | source)
XLA Modules:
  0.0 67.3 jit_solution(8568901555101577674)
XLA Ops:
  0.0 66.7 %shard_map.73 = bf16[64,256]{1,0:T(8,128)(2,1)S(1)} custom-call(s32[128]{0:T(128)} %roots_hbm.1, s32[3,16]{1,0:T(4,128)} %parents_hbm.1, s32[8,16]{1,0:T(8,128)} %bitcast.7, bf16[64,256]{1,0:T(8,128)(2,1)} %bitcast.6, bf16[64,2048]{1,0:T(8,128)(2,1)} %bitcast.5, bf16[1024,2048]{1,0:T(8,128)(2,1)} %prompt_hbm.1, bf16[16,32,2048]{2,1,0:T(8,128)(2,1)} %suffix_hbm.1), custom_call_target="tpu_custom_call" | custom-call | flops 3300000000 | bytes 7000000 | tf_op jit(solution)/shard_map/pallas_call | solution.py:397
  66.7 0.6 copy.9

commit v3 on v2

v3 whole, which is shorter than its diff:
```python
import functools
import math

import jax
import jax.numpy as jnp
from jax import lax
from jax.experimental import pallas as pl
from jax.experimental.pallas import tpu as pltpu
from jax.sharding import PartitionSpec as P

MESH = pl.DeviceIdType.MESH

QUERY_HEAD_COUNT = 64
KEY_VALUE_HEADS = 8
HEAD_SIZE = 128
DRAFT_STEPS = 4
WIDTH = KEY_VALUE_HEADS * HEAD_SIZE
REQ = 8
CTX = 32
CHIPS = CTX // 2
LAST = KEY_VALUE_HEADS - 1
EARLY = 4
PER_REQ = 16
CAP = 2
SPAN = 32
PROMPT = 1024
TOKENS = DRAFT_STEPS * PER_REQ
ROWS = 2 * TOKENS
OWNERS = CTX // KEY_VALUE_HEADS
STAT = 8
MASKED = -1e30
EXP_SCALE = math.log2(math.e) / math.sqrt(HEAD_SIZE)


def nt_dot(a, b):
    return lax.dot_general(a, b, (((1,), (1,)), ((), ())), preferred_element_type=jnp.float32)


def kernel(
    roots_hbm, parents_hbm, mask_hbm, queries_hbm, draft_hbm, prompt_hbm, suffix_hbm, out_ref,
    prompt, suffix, first_pieces, draft, query_in, zsend, zrecv, query_all, xsend, xrecv, keep, rsend, rrecv,
    last_part, lsend, lrecv, base, mask,
    roots, parents, block_mask, pick, slot,
    load_sem, zs_sem, zr_sem, qs_sem, qf_sem, qr_sem, xs_sem, xr_sem, rs_sem, rr_sem, ls_sem, lr_sem,
):
    z = lax.axis_index("req")
    c = lax.axis_index("ctx")
    group = c // OWNERS
    chip = c // 2
    core = lax.rem(c, 2)
    sibling = chip * 2 + 1 - core
    place = lax.rem(c, OWNERS)
    across = group * OWNERS + OWNERS - 1 - place

    def head_of(k):
        return lax.rem(group + 1 + k, KEY_VALUE_HEADS)

    def columns(k):
        key_at = pl.ds(pl.multiple_of(head_of(k) * HEAD_SIZE, HEAD_SIZE), HEAD_SIZE)
        value_at = pl.ds(pl.multiple_of(WIDTH + head_of(k) * HEAD_SIZE, HEAD_SIZE), HEAD_SIZE)
        return key_at, value_at

    load_roots = pltpu.make_async_copy(roots_hbm, roots, load_sem.at[0])
    load_roots.start()
    key_at, value_at = columns(0)
    load_keys = pltpu.make_async_copy(suffix_hbm.at[:, :, key_at], first_pieces.at[0], load_sem.at[1])
    load_values = pltpu.make_async_copy(suffix_hbm.at[:, :, value_at], first_pieces.at[1], load_sem.at[2])
    load_keys.start()
    load_values.start()

    barrier = pltpu.get_barrier_semaphore()

    def greet_z(i, _):
        pl.semaphore_signal(barrier, inc=1, device_id=(lax.rem(z + i, REQ), c), device_id_type=MESH)
        return 0

    def greet_chip(i, _):
        to = lax.rem(chip + i, CHIPS) * 2 + core
        pl.semaphore_signal(barrier, inc=1, device_id=(z, to), device_id_type=MESH)
        return 0

    lax.fori_loop(1, REQ, greet_z, 0)
    lax.fori_loop(1, CHIPS, greet_chip, 0)
    pl.semaphore_signal(barrier, inc=1, device_id=(z, sibling), device_id_type=MESH)
    pl.semaphore_signal(barrier, inc=1, device_id=(z, across), device_id_type=MESH)

    load_query = pltpu.make_async_copy(queries_hbm, query_in, load_sem.at[3])
    load_suffix = pltpu.make_async_copy(suffix_hbm, suffix, load_sem.at[4])
    load_parents = pltpu.make_async_copy(parents_hbm, parents, load_sem.at[5])
    load_mask = pltpu.make_async_copy(mask_hbm, block_mask, load_sem.at[6])
    load_prompt = pltpu.make_async_copy(prompt_hbm, prompt, load_sem.at[7])
    load_draft = pltpu.make_async_copy(draft_hbm, draft, load_sem.at[8])
    load_query.start()
    load_suffix.start()
    load_parents.start()
    load_mask.start()
    load_prompt.start()
    load_draft.start()

    def choose(d, _):
        count, first, second = jnp.int32(0), jnp.int32(0), jnp.int32(0)
        for j in range(PER_REQ):
            root = roots[d * PER_REQ + j]
            mine = (root >> 4) == z
            local = root & 15
            first = jnp.where(mine & (count == 0), local, first)
            second = jnp.where(mine & (count == 1), local, second)
            count = count + mine.astype(jnp.int32)
        pick[2 * d] = first
        pick[2 * d + 1] = second
        return 0

    load_roots.wait()
    lax.fori_loop(0, REQ, choose, 0)

    def pack(k, keys_of, values_of):
        def one(d, _):
            for s in range(CAP):
                index = pick[2 * d + s]
                zsend[k, d, 0, s * SPAN : (s + 1) * SPAN, :] = keys_of(index)
                zsend[k, d, 1, s * SPAN : (s + 1) * SPAN, :] = values_of(index)
            return 0

        lax.fori_loop(0, REQ, one, 0)

    def z_copy(k, i):
        d = lax.rem(z + i, REQ)
        return pltpu.make_async_remote_copy(
            src_ref=zsend.at[k, d],
            dst_ref=zrecv.at[k, z],
            send_sem=zs_sem.at[k, d],
            recv_sem=zr_sem.at[k, z],
            device_id=(d, c),
            device_id_type=MESH,
        )

    def z_arrival(k, i):
        s = lax.rem(z + i, REQ)
        return pltpu.make_async_remote_copy(
            src_ref=zsend.at[k, s],
            dst_ref=zrecv.at[k, s],
            send_sem=zs_sem.at[k, s],
            recv_sem=zr_sem.at[k, s],
            device_id=(s, c),
            device_id_type=MESH,
        )

    def q_send(source, to, sem):
        return pltpu.make_async_remote_copy(
            src_ref=query_all.at[source],
            dst_ref=query_all.at[source],
            send_sem=sem,
            recv_sem=qr_sem.at[source],
            device_id=(z, to),
            device_id_type=MESH,
        )

    def q_copy(to):
        return q_send(c, to, qs_sem.at[to])

    def q_forward(source):
        return q_send(source, sibling, qf_sem.at[source])

    def x_copy(k, half):
        return pltpu.make_async_remote_copy(
            src_ref=xsend.at[k, half],
            dst_ref=xrecv.at[k, half],
            send_sem=xs_sem.at[k, half],
            recv_sem=xr_sem.at[k, half],
            device_id=(z, sibling),
            device_id_type=MESH,
        )

    def r_copy(to_chip):
        spot = lax.rem(chip - to_chip // 2 * 2 + 2 * CHIPS - 2, CHIPS)
        return pltpu.make_async_remote_copy(
            src_ref=rsend.at[to_chip],
            dst_ref=rrecv.at[spot],
            send_sem=rs_sem.at[to_chip],
            recv_sem=rr_sem.at[spot],
            device_id=(z, to_chip * 2 + core),
            device_id_type=MESH,
        )

    def r_arrival(spot):
        from_chip = lax.rem(group * 2 + 2 + spot, CHIPS)
        return pltpu.make_async_remote_copy(
            src_ref=rsend.at[from_chip],
            dst_ref=rrecv.at[spot],
            send_sem=rs_sem.at[from_chip],
            recv_sem=rr_sem.at[spot],
            device_id=(z, from_chip * 2 + core),
            device_id_type=MESH,
        )

    def l_copy(to):
        return pltpu.make_async_remote_copy(
            src_ref=lsend.at[to],
            dst_ref=lrecv.at[place],
            send_sem=ls_sem.at[to],
            recv_sem=lr_sem.at[place],
            device_id=(z, group * OWNERS + to),
            device_id_type=MESH,
        )

    def l_arrival(source):
        return pltpu.make_async_remote_copy(
            src_ref=lsend.at[source],
            dst_ref=lrecv.at[source],
            send_sem=ls_sem.at[source],
            recv_sem=lr_sem.at[source],
            device_id=(z, group * OWNERS + source),
            device_id_type=MESH,
        )

    def send_stage(k):
        for i in (4, 3, 5, 2, 6, 1, 7):
            z_copy(k, i).start()

    load_keys.wait()
    load_values.wait()
    pack(0, lambda index: first_pieces[0, index], lambda index: first_pieces[1, index])
    pl.semaphore_wait(barrier, REQ - 1 + CHIPS + 1)
    send_stage(0)
    zrecv[0, z] = zsend[0, z]

    load_query.wait()
    query_all[c, 0:TOKENS, :] = query_in[:, 0:HEAD_SIZE]
    query_all[c, TOKENS:ROWS, :] = query_in[:, HEAD_SIZE : 2 * HEAD_SIZE]

    q_copy(sibling).start()

    def send_query(i, _):
        to = lax.rem(group + 2 * KEY_VALUE_HEADS - 1 - i // 2, KEY_VALUE_HEADS) * 2 + lax.rem(chip + i, 2)

        @pl.when(to != chip)
        def _():
            q_copy(to * 2 + core).start()

        return 0

    lax.fori_loop(0, CHIPS, send_query, 0)

    load_suffix.wait()

    def pack_and_send(k, _):
        key_at, value_at = columns(k)
        pack(k, lambda index: suffix[index, :, key_at], lambda index: suffix[index, :, value_at])
        send_stage(k)
        zrecv[k, z] = zsend[k, z]
        return 0

    lax.fori_loop(1, KEY_VALUE_HEADS, pack_and_send, 0)

    load_parents.wait()
    load_mask.wait()

    own = [roots[z * PER_REQ + j] >> 4 for j in range(PER_REQ)]
    for j in range(PER_REQ):
        rank = jnp.int32(0)
        for i in range(j):
            rank = rank + (own[i] == own[j]).astype(jnp.int32)
        slot[j] = own[j] * CAP + rank

    lane_slot = lax.broadcasted_iota(jnp.int32, (1, REQ * CAP * SPAN), 1) // SPAN
    lane_token = lax.rem(lax.broadcasted_iota(jnp.int32, (1, ROWS), 1), TOKENS)

    def trace(j, carry):
        lines = list(carry)
        for t in range(DRAFT_STEPS):
            at = j
            path = {t: at}
            for back in range(t - 1, -1, -1):
                at = parents[back, at]
                path[back] = at
            here = jnp.where(block_mask[group, at] > 0, slot[at], -1)
            mask[pl.ds(t * PER_REQ + j, 1), :] = jnp.where(lane_slot == here, 0.0, MASKED)
            for s in range(t + 1):
                lines[s] = jnp.where(lane_token == t * PER_REQ + j, path[s], lines[s])
        return tuple(lines)

    lines = lax.fori_loop(
        0, PER_REQ, trace, tuple(jnp.full((1, ROWS), -1, jnp.int32) for _ in range(DRAFT_STEPS))
    )

    load_prompt.wait()
    load_draft.wait()
    lane = lax.broadcasted_iota(jnp.int32, (ROWS, HEAD_SIZE), 1)

    def hand_on(k):
        for half in range(2):
            owner = head_of(k) * OWNERS + core + 2 * half

            @pl.when(owner != c)
            def _():
                q_send(owner, sibling, qf_sem.at[owner]).wait_recv()
                q_forward(owner).start()

    def weigh(scores, peak, values):
        weight = jnp.exp2((scores - peak) * EXP_SCALE)
        total = jnp.sum(weight, axis=1, keepdims=True)
        return total, jnp.dot(weight.astype(jnp.bfloat16), values, preferred_element_type=jnp.float32)

    def suffix_scores(k, rows):
        keys = zrecv[k, :, 0].reshape(REQ * CAP * SPAN, HEAD_SIZE)
        bias = mask[...]
        return nt_dot(rows, keys) + jnp.concatenate([bias, bias], axis=0)

    def suffix_values(k):
        return zrecv[k, :, 1].reshape(REQ * CAP * SPAN, HEAD_SIZE)

    def partial(k, owner):
        key_at, value_at = columns(k)
        rows = query_all[owner]
        score_prompt = nt_dot(rows, prompt[:, key_at])
        score_suffix = suffix_scores(k, rows)
        peak = jnp.maximum(
            jnp.max(score_prompt, axis=1, keepdims=True), jnp.max(score_suffix, axis=1, keepdims=True)
        )
        total_prompt, accum_prompt = weigh(score_prompt, peak, prompt[:, value_at])
        total_suffix, accum_suffix = weigh(score_suffix, peak, suffix_values(k))
        return accum_prompt + accum_suffix, jnp.where(lane == 0, peak, total_prompt + total_suffix)

    def wait_z(k):
        def one(i, _):
            z_arrival(k, i).wait_recv()
            return 0

        lax.fori_loop(1, REQ, one, 0)

    def combine(k):
        def one(half, _):
            to_chip = head_of(k) * 2 + half
            x_copy(k, half).wait_recv()
            peak_here, peak_there = keep[lax.rem(k, 2), half, ROWS : 2 * ROWS, 0:1], xrecv[k, half, ROWS : 2 * ROWS, 0:1]
            total_here, total_there = keep[lax.rem(k, 2), half, ROWS : 2 * ROWS, 1:2], xrecv[k, half, ROWS : 2 * ROWS, 1:2]
            peak = jnp.maximum(peak_here, peak_there)
            here = jnp.exp2((peak_here - peak) * EXP_SCALE)
            there = jnp.exp2((peak_there - peak) * EXP_SCALE)
            rsend[to_chip, 0:ROWS, :] = keep[lax.rem(k, 2), half, 0:ROWS, :] * here + xrecv[k, half, 0:ROWS, :] * there
            stats = jnp.transpose(jnp.where(lane == 0, peak, total_here * here + total_there * there))
            rsend[to_chip, ROWS : ROWS + STAT, :] = stats[0:STAT]

            r_copy(to_chip).start()
            return 0

        lax.fori_loop(0, 2, one, 0)

    def last_prompt(part):
        owner = group * OWNERS + part

        @pl.when(lax.rem(part, 2) != core)
        def _():
            q_send(owner, sibling, qf_sem.at[owner]).wait_recv()

        score_prompt = nt_dot(query_all[owner], prompt[:, columns(LAST)[0]])
        peak = jnp.max(score_prompt, axis=1, keepdims=True)
        total, accum = weigh(score_prompt, peak, prompt[:, columns(LAST)[1]])
        last_part[part, 0:ROWS, :] = accum
        last_part[part, ROWS : 2 * ROWS, :] = jnp.where(lane == 0, peak, total)

    def add_early():
        def wait_r(spot, _):
            r_arrival(spot).wait_recv()
            return 0

        lax.fori_loop(EARLY, CHIPS - 2, wait_r, 0)
        peaks = rrecv[EARLY : CHIPS - 2, ROWS, :]
        peak = jnp.max(peaks, axis=0, keepdims=True)
        factor = jnp.exp2((peaks - peak) * EXP_SCALE)
        total = jnp.sum(rrecv[EARLY : CHIPS - 2, ROWS + 1, :] * factor, axis=0, keepdims=True)
        turned = jnp.transpose(
            jnp.concatenate([factor, jnp.broadcast_to(total, (ROWS - CHIPS + 2 + EARLY, ROWS))], axis=0)
        )
        numerator = rrecv[EARLY, 0:ROWS, :] * turned[:, 0:1]
        for s in range(EARLY + 1, CHIPS - 2):
            numerator = numerator + rrecv[s, 0:ROWS, :] * turned[:, s - EARLY : s - EARLY + 1]
        base[0:ROWS, :] = numerator
        base[ROWS : ROWS + 1, :] = peak
        base[ROWS + 1 : ROWS + 2, :] = total

    def stage(k, _):
        @pl.when(k < LAST - 1)
        def _():
            hand_on(k + 1)

        @pl.when(k > 0)
        def _():
            combine(k - 1)

        @pl.when(k == 1)
        def _():
            hand_on(LAST)

        @pl.when((k > 1) & (k < 2 + OWNERS))
        def _():
            last_prompt(k - 2)

        @pl.when(k == LAST - 1)
        def _():
            add_early()

        wait_z(k)

        def give(half, _):
            owner = head_of(k) * OWNERS + 1 - core + 2 * half
            q_send(owner, sibling, qf_sem.at[owner]).wait_recv()
            accum, stats = partial(k, owner)
            xsend[k, half, 0:ROWS, :] = accum
            xsend[k, half, ROWS : 2 * ROWS, :] = stats
            x_copy(k, half).start()
            return 0

        lax.fori_loop(0, 2, give, 0)

        def hold(half, _):
            accum, stats = partial(k, head_of(k) * OWNERS + core + 2 * half)
            keep[lax.rem(k, 2), half, 0:ROWS, :] = accum
            keep[lax.rem(k, 2), half, ROWS : 2 * ROWS, :] = stats
            return 0

        lax.fori_loop(0, 2, hold, 0)

        return 0

    hand_on(0)
    lax.fori_loop(0, LAST, stage, 0)
    combine(LAST - 1)

    key_at, value_at = columns(LAST)

    score_draft = nt_dot(draft[:, key_at], query_all[c])
    particle = lax.broadcasted_iota(jnp.int32, (PER_REQ, ROWS), 0)
    allowed = jnp.concatenate([jnp.where(particle == line, 1, 0) for line in lines], axis=0)
    score_draft = jnp.where(allowed > 0, score_draft, MASKED)

    wait_z(LAST)

    def last_suffix(i, _):
        part = lax.rem(place + OWNERS - 1 - i, OWNERS)
        score_suffix = suffix_scores(LAST, query_all[group * OWNERS + part])
        peak_prompt, total_prompt = last_part[part, ROWS : 2 * ROWS, 0:1], last_part[part, ROWS : 2 * ROWS, 1:2]
        peak = jnp.maximum(peak_prompt, jnp.max(score_suffix, axis=1, keepdims=True))
        total, accum = weigh(score_suffix, peak, suffix_values(LAST))
        carried = jnp.exp2((peak_prompt - peak) * EXP_SCALE)
        lsend[part, 0:ROWS, :] = accum + last_part[part, 0:ROWS, :] * carried
        stats = jnp.transpose(jnp.where(lane == 0, peak, total + total_prompt * carried))
        lsend[part, ROWS : ROWS + STAT, :] = stats[0:STAT]

        @pl.when(part != place)
        def _():
            l_copy(part).start()

        return 0

    lax.fori_loop(0, OWNERS, last_suffix, 0)

    for spot in range(EARLY):
        r_arrival(spot).wait_recv()

    def drain_z(k):
        def one(i, _):
            z_copy(k, i).wait_send()
            return 0

        lax.fori_loop(1, REQ, one, 0)

    def drain_stage(k, _):
        drain_z(k)
        for half in range(2):
            x_copy(k, half).wait_send()
            r_copy(head_of(k) * 2 + half).wait_send()
        return 0

    lax.fori_loop(0, LAST, drain_stage, 0)

    def drain_chip(i, _):
        to = lax.rem(chip + i, CHIPS)
        q_copy(to * 2 + core).wait_send()
        q_forward(to * 2 + core).wait_send()
        return 0

    lax.fori_loop(1, CHIPS, drain_chip, 0)
    q_copy(sibling).wait_send()

    lrecv[place] = lsend[place]
    drain_z(LAST)
    for i in range(1, OWNERS):
        l_arrival(lax.rem(place + i, OWNERS)).wait_recv()

    base_peak, base_total = base[ROWS : ROWS + 1, :], base[ROWS + 1 : ROWS + 2, :]
    peaks = jnp.concatenate([lrecv[:, ROWS, :], rrecv[0:EARLY, ROWS, :], base_peak], axis=0)
    totals = jnp.concatenate([lrecv[:, ROWS + 1, :], rrecv[0:EARLY, ROWS + 1, :], base_total], axis=0)
    highest = jnp.maximum(jnp.max(peaks, axis=0, keepdims=True), jnp.max(score_draft, axis=0, keepdims=True))
    factor = jnp.exp2((peaks - highest) * EXP_SCALE)
    weight_draft = jnp.exp2((score_draft - highest) * EXP_SCALE)
    total = jnp.sum(totals * factor, axis=0, keepdims=True) + jnp.sum(weight_draft, axis=0, keepdims=True)
    count = OWNERS + EARLY + 1
    turned = jnp.transpose(
        jnp.concatenate([factor, jnp.broadcast_to(total, (TOKENS - count, ROWS)), weight_draft], axis=0)
    )
    numerator = jnp.dot(
        turned[:, TOKENS:].astype(jnp.bfloat16), draft[:, value_at], preferred_element_type=jnp.float32
    )
    for s in range(OWNERS):
        numerator = numerator + lrecv[s, 0:ROWS, :] * turned[:, s : s + 1]
    for s in range(EARLY):
        numerator = numerator + rrecv[s, 0:ROWS, :] * turned[:, OWNERS + s : OWNERS + s + 1]
    numerator = numerator + base[0:ROWS, :] * turned[:, count - 1 : count]
    result = (numerator / turned[:, count : count + 1]).astype(jnp.bfloat16)
    out_ref[:, 0:HEAD_SIZE] = result[0:TOKENS]
    out_ref[:, HEAD_SIZE : 2 * HEAD_SIZE] = result[TOKENS:ROWS]
    for i in range(1, OWNERS):
        l_copy(lax.rem(place + i, OWNERS)).wait_send()


def body(prompt_key_value, suffix_key_value, roots, parents, block_mask, queries, draft_kv):
    hbm = pl.BlockSpec(memory_space=pltpu.HBM)
    bf16, f32 = jnp.bfloat16, jnp.float32
    result = pl.pallas_call(
        kernel,
        out_shape=jax.ShapeDtypeStruct((TOKENS, 2 * HEAD_SIZE), bf16),
        in_specs=[hbm] * 7,
        out_specs=pl.BlockSpec(memory_space=pltpu.VMEM),
        scratch_shapes=[
            pltpu.VMEM((PROMPT, 2 * WIDTH), bf16),
            pltpu.VMEM((PER_REQ, SPAN, 2 * WIDTH), bf16),
            pltpu.VMEM((2, PER_REQ, SPAN, HEAD_SIZE), bf16),
            pltpu.VMEM((TOKENS, 2 * WIDTH), bf16),
            pltpu.VMEM((TOKENS, 2 * HEAD_SIZE), bf16),
            pltpu.VMEM((KEY_VALUE_HEADS, REQ, 2, CAP * SPAN, HEAD_SIZE), bf16),
            pltpu.VMEM((KEY_VALUE_HEADS, REQ, 2, CAP * SPAN, HEAD_SIZE), bf16),
            pltpu.VMEM((CTX, ROWS, HEAD_SIZE), bf16),
            pltpu.VMEM((LAST, 2, 2 * ROWS, HEAD_SIZE), f32),
            pltpu.VMEM((LAST, 2, 2 * ROWS, HEAD_SIZE), f32),
            pltpu.VMEM((2, 2, 2 * ROWS, HEAD_SIZE), f32),
            pltpu.VMEM((CHIPS, ROWS + STAT, HEAD_SIZE), f32),
            pltpu.VMEM((CHIPS - 2, ROWS + STAT, HEAD_SIZE), f32),
            pltpu.VMEM((OWNERS, 2 * ROWS, HEAD_SIZE), f32),
            pltpu.VMEM((OWNERS, ROWS + STAT, HEAD_SIZE), f32),
            pltpu.VMEM((OWNERS, ROWS + STAT, HEAD_SIZE), f32),
            pltpu.VMEM((ROWS + STAT, HEAD_SIZE), f32),
            pltpu.VMEM((TOKENS, REQ * CAP * SPAN), f32),
            pltpu.SMEM((REQ * PER_REQ,), jnp.int32),
            pltpu.SMEM((DRAFT_STEPS - 1, PER_REQ), jnp.int32),
            pltpu.SMEM((KEY_VALUE_HEADS, PER_REQ), jnp.int32),
            pltpu.SMEM((REQ * CAP,), jnp.int32),
            pltpu.SMEM((PER_REQ,), jnp.int32),
            pltpu.SemaphoreType.DMA((9,)),
            pltpu.SemaphoreType.DMA((KEY_VALUE_HEADS, REQ)),
            pltpu.SemaphoreType.DMA((KEY_VALUE_HEADS, REQ)),
            pltpu.SemaphoreType.DMA((CTX,)),
            pltpu.SemaphoreType.DMA((CTX,)),
            pltpu.SemaphoreType.DMA((CTX,)),
            pltpu.SemaphoreType.DMA((LAST, 2)),
            pltpu.SemaphoreType.DMA((LAST, 2)),
            pltpu.SemaphoreType.DMA((CHIPS,)),
            pltpu.SemaphoreType.DMA((CHIPS - 2,)),
            pltpu.SemaphoreType.DMA((OWNERS,)),
            pltpu.SemaphoreType.DMA((OWNERS,)),
        ],
        compiler_params=pltpu.CompilerParams(
            collective_id=0, has_side_effects=True, vmem_limit_bytes=48 * 1024 * 1024
        ),
        cost_estimate=pl.CostEstimate(flops=3_300_000_000, bytes_accessed=7_000_000, transcendentals=6_300_000),
    )(*(
        pltpu.with_memory_space_constraint(operand, pltpu.HBM)
        for operand in (
            roots,
            parents,
            block_mask.T,
            queries.reshape(TOKENS, 2 * HEAD_SIZE),
            draft_kv.reshape(TOKENS, 2 * WIDTH),
            prompt_key_value,
            suffix_key_value,
        )
    ))
    return result.reshape(DRAFT_STEPS, PER_REQ, 2 * HEAD_SIZE)


def solution(mesh):
    return jax.shard_map(
        body,
        mesh=mesh,
        in_specs=(
            P("ctx", None),
            P("req", "ctx", None),
            P(),
            P(None, "req"),
            P("req", None),
            P(None, "req", "ctx"),
            P(None, "req", None),
        ),
        out_specs=P(None, "req", "ctx"),
        check_vma=False,
    )
```

time: 67.9 us -> 66.3 us (0.976)
  Pallas kernels: 66.7 us -> 65.6 us
    pallas_call x1, Pallas kernels: 66.7 us -> 65.6 us  [body(): pl.pallas_call(kernel, out_shape=jax.ShapeDtypeStruct((TOKENS, 2 * HEAD_S...]
where the time goes in v3:
time: 66.3 us
  Pallas kernels  65.6 us (99%)
    pallas_call x1, Pallas kernels, body(): pl.pallas_call(kernel, out_shape=jax.ShapeDtypeStruct((TOKENS, 2 * HEAD_S...  65.6 us

profile of v3, /device:TPU:1, one launch (start us, length us, event | category | flops | bytes accessed | tf_op | source)
XLA Modules:
  0.0 66.3 jit_solution(1444406937569095470)
XLA Ops:
  0.0 65.6 %shard_map.73 = bf16[64,256]{1,0:T(8,128)(2,1)S(1)} custom-call(s32[128]{0:T(128)} %roots_hbm.1, s32[3,16]{1,0:T(4,128)} %parents_hbm.1, s32[8,16]{1,0:T(8,128)} %bitcast.7, bf16[64,256]{1,0:T(8,128)(2,1)} %bitcast.6, bf16[64,2048]{1,0:T(8,128)(2,1)} %bitcast.5, bf16[1024,2048]{1,0:T(8,128)(2,1)} %prompt_hbm.1, bf16[16,32,2048]{2,1,0:T(8,128)(2,1)} %suffix_hbm.1), custom_call_target="tpu_custom_call" | custom-call | flops 3300000000 | bytes 7000000 | tf_op jit(solution)/shard_map/pallas_call | solution.py:520
  65.6 0.6 copy.9

commit v4 on v3

--- a/solution.py
+++ b/solution.py
@@ -91,11 +91,8 @@
     load_prompt = pltpu.make_async_copy(prompt_hbm, prompt, load_sem.at[7])
     load_draft = pltpu.make_async_copy(draft_hbm, draft, load_sem.at[8])
     load_query.start()
-    load_suffix.start()
     load_parents.start()
     load_mask.start()
-    load_prompt.start()
-    load_draft.start()
 
     def choose(d, _):
         count, first, second = jnp.int32(0), jnp.int32(0), jnp.int32(0)
@@ -222,6 +219,9 @@
     pack(0, lambda index: first_pieces[0, index], lambda index: first_pieces[1, index])
     pl.semaphore_wait(barrier, REQ - 1 + CHIPS + 1)
     send_stage(0)
+    load_suffix.start()
+    load_prompt.start()
+    load_draft.start()
     zrecv[0, z] = zsend[0, z]
 
     load_query.wait()

time: 66.3 us -> 66.3 us (level)
  no operation moved by 1% of the time
where the time goes in v4:
time: 66.3 us
  Pallas kernels  65.6 us (99%)
    pallas_call x1, Pallas kernels, body(): pl.pallas_call(kernel, out_shape=jax.ShapeDtypeStruct((TOKENS, 2 * HEAD_S...  65.6 us

profile of v4, /device:TPU:1, one launch (start us, length us, event | category | flops | bytes accessed | tf_op | source)
XLA Modules:
  0.0 66.3 jit_solution(6596684971334826510)
XLA Ops:
  0.0 65.6 %shard_map.73 = bf16[64,256]{1,0:T(8,128)(2,1)S(1)} custom-call(s32[128]{0:T(128)} %roots_hbm.1, s32[3,16]{1,0:T(4,128)} %parents_hbm.1, s32[8,16]{1,0:T(8,128)} %bitcast.7, bf16[64,256]{1,0:T(8,128)(2,1)} %bitcast.6, bf16[64,2048]{1,0:T(8,128)(2,1)} %bitcast.5, bf16[1024,2048]{1,0:T(8,128)(2,1)} %prompt_hbm.1, bf16[16,32,2048]{2,1,0:T(8,128)(2,1)} %suffix_hbm.1), custom_call_target="tpu_custom_call" | custom-call | flops 3300000000 | bytes 7000000 | tf_op jit(solution)/shard_map/pallas_call | solution.py:520
  65.6 0.6 copy.9
